TPU v7x, 256 devices: a whole 4x4x8 slice. The times are simulated.
256 devices in a mesh: cfg: 2 (over y_lo), req: 8 (over x, core), seq: 16 (over z, y_hi).
Axes of the slice: x: 4, y: 4 (y_hi: 2, y_lo: 2; y = y_hi * 2 + y_lo), z: 8, core: 2. Of those that a mesh axis runs over, the one named last changes fastest.
Arguments:
- image_hidden: bfloat16 [2, 8, 2048, 1536], P('cfg', 'req', 'seq'), may hold values from -6 to 6
- text_hidden: bfloat16 [2, 8, 160, 1536], P('cfg', 'req', 'seq'), may hold values from -6 to 6
- modulation: float32 [2, 8, 10, 1536], P('cfg', 'req'), may hold values from -3 to 3
- attn_weight: bfloat16 [1536, 5120], P(None, 'seq'), may hold values from -8 to 8
- proj_weight: bfloat16 [1024, 1536], replicated, may hold values from -0.1875 to 0.1875
- mlp_in_weight: bfloat16 [1536, 6144], P(None, 'seq'), may hold values from -0.15625 to 0.15625
- mlp_out_weight: bfloat16 [6144, 1536], P('seq'), may hold values from -0.078125 to 0.078125
- final_weight: bfloat16 [64, 1536], replicated, may hold values from -0.15625 to 0.15625
- latents: float32 [8, 64, 2048], P('req', 'cfg', 'seq'), may hold values from -6 to 6
- guidance: float32 [8], P('req'), may hold values from 3 to 7
- text_lengths: int32 [2, 8], P('cfg', 'req'), may hold values from 1 to 154, 693 in all within a row
- step_index: int32 [8], P('req'), may hold values from 0 to 27
- step_count: int32 [8], P('req'), may hold values from 1 to 3
Outputs:
- velocity: float32 [8, 64, 2048], P('req', 'cfg', 'seq')
- new_latents: float32 [8, 64, 2048], P('req', 'cfg', 'seq')
All inputs are finite; a program needn't handle non-finite values. No bound on the sum of `text_lengths` on one device may be relied on, other than what follows from the above.
Results may differ from a plain program's by a relative error of at most 0.017.
Values may be sent and summed in bfloat16 or wider, within the bound.
No kernel may reach another device: no remote copies, remote signals or barrier semaphores. Data moves between devices by JAX's collectives and lax.ppermute only.
A program may use at most 128 MiB of HBM per device.

v0:
```python
import jax
import jax.numpy as jnp
from jax import lax
from jax.sharding import PartitionSpec as P

HEADS = 16
HEAD = 64
STEPS = 28
EPS_NORM = 1e-06


def partner(value, axis, distance):
    mask = 2**distance
    pairs = [(source, source ^ mask) for source in range(lax.axis_size(axis))]
    return lax.ppermute(value, axis, pairs)


def modulate(rows_in, scale_row, shift_row):
    values = rows_in.astype(jnp.float32)
    center = jnp.mean(values, axis=-1, keepdims=True)
    spread = jnp.mean(jnp.square(values - center), axis=-1, keepdims=True)
    return (
        (values - center) * lax.rsqrt(spread + EPS_NORM) * (1.0 + scale_row) + shift_row
    ).astype(jnp.bfloat16)


def sigma_of(index):
    remain = 1.0 - index.astype(jnp.float32) / STEPS
    return 3.0 * remain / (1.0 + 2.0 * remain)


def split_columns(weight_piece):
    width_in = weight_piece.shape[0]
    head_count = weight_piece.shape[1] // (5 * HEAD)
    shaped = weight_piece.reshape(width_in, head_count, 5, HEAD)
    image_cols = shaped[:, :, 0:3, :].reshape(width_in, head_count * 3 * HEAD)
    text_cols = shaped[:, :, 3:5, :].reshape(width_in, head_count * 2 * HEAD)
    return (image_cols, text_cols)


def local(
    image_hidden,
    text_hidden,
    modulation,
    attn_weight,
    proj_weight,
    mlp_in_weight,
    mlp_out_weight,
    final_weight,
    latents,
    guidance,
    text_lengths,
    step_index,
    step_count,
):
    seq_size = lax.axis_size("seq")
    local_heads = HEADS // seq_size
    image_rows = image_hidden[0, 0]
    text_rows = text_hidden[0, 0]
    mod_rows = modulation[0, 0]
    local_rows = image_rows.shape[0]
    image_total = local_rows * seq_size
    text_total = text_rows.shape[0] * seq_size
    image_norm = modulate(image_rows, mod_rows[1], mod_rows[0])
    text_norm = modulate(text_rows, mod_rows[4], mod_rows[3])
    image_cols, text_cols = split_columns(lax.all_gather(attn_weight, "seq", axis=1, tiled=True))
    image_part = jnp.dot(image_norm, image_cols, preferred_element_type=jnp.float32).astype(
        jnp.bfloat16
    )
    text_part = jnp.dot(text_norm, text_cols, preferred_element_type=jnp.float32).astype(
        jnp.bfloat16
    )
    image_qkv = image_part
    text_kv = text_part
    image_qkv, text_kv = (
        lax.all_to_all(image_qkv, "seq", split_axis=1, concat_axis=0, tiled=True),
        lax.all_to_all(text_kv, "seq", split_axis=1, concat_axis=0, tiled=True),
    )
    image_qkv = image_qkv.reshape(image_total, local_heads, 3, HEAD)
    text_kv = text_kv.reshape(text_total, local_heads, 2, HEAD)
    keys_all = jnp.concatenate([image_qkv[:, :, 1], text_kv[:, :, 0]], axis=0)
    values_all = jnp.concatenate([image_qkv[:, :, 2], text_kv[:, :, 1]], axis=0)
    slots = jnp.arange(text_total, dtype=jnp.int32)
    valid = jnp.concatenate([jnp.ones((image_total,), dtype=bool), slots < text_lengths[0, 0]])
    block_rows = local_rows
    while block_rows < 512 and image_total % (block_rows * 2) == 0:
        block_rows = block_rows * 2
    block_total = image_total // block_rows
    query_blocks = image_qkv[:, :, 0].reshape(block_total, block_rows, local_heads, HEAD)

    def attend(query_block):
        scores = jnp.einsum(
            "qhe,khe->hqk", query_block, keys_all, preferred_element_type=jnp.float32
        ) * HEAD ** (-0.5)
        scores = jnp.where(valid[None, None, :], scores, -1e30)
        row_max = jnp.max(scores, axis=2, keepdims=True)
        weights = jnp.exp(scores - row_max)
        total = jnp.sum(weights, axis=2, keepdims=True)
        probs = weights.astype(jnp.bfloat16)
        mixed = (
            jnp.einsum("hqk,khe->hqe", probs, values_all, preferred_element_type=jnp.float32)
            / total
        )
        return jnp.transpose(mixed.astype(jnp.bfloat16), (1, 0, 2))

    attended = lax.map(attend, query_blocks).reshape(image_total, local_heads * HEAD)
    attended = lax.all_to_all(attended, "seq", split_axis=0, concat_axis=1, tiled=True)
    hidden = image_rows.astype(jnp.float32) + mod_rows[2] * jnp.dot(
        attended, proj_weight, preferred_element_type=jnp.float32
    )
    mlp_norm = modulate(hidden, mod_rows[8], mod_rows[7])
    mlp_all = lax.all_gather(mlp_norm, "seq", axis=0, tiled=True)
    inner = jax.nn.gelu(
        jnp.dot(mlp_all, mlp_in_weight, preferred_element_type=jnp.float32), approximate=True
    ).astype(jnp.bfloat16)
    mlp_out = lax.psum_scatter(
        jnp.dot(inner, mlp_out_weight, preferred_element_type=jnp.float32).astype(jnp.bfloat16),
        "seq",
        scatter_dimension=0,
        tiled=True,
    ).astype(jnp.float32)
    block_out = hidden + mod_rows[9] * mlp_out
    final_norm = modulate(block_out, mod_rows[6], mod_rows[5])
    own_vel = lax.dot_general(
        final_weight, final_norm, (((1,), (1,)), ((), ())), preferred_element_type=jnp.float32
    )
    partner_vel = partner(own_vel.astype(jnp.bfloat16), "cfg", 0).astype(own_vel.dtype)
    leading = lax.axis_index("cfg") == 0
    cond_vel = jnp.where(leading, own_vel, partner_vel)
    uncond_vel = jnp.where(leading, partner_vel, own_vel)
    guided = uncond_vel + guidance[0] * (cond_vel - uncond_vel)
    cond_sq, guided_sq = lax.psum((jnp.sum(cond_vel * cond_vel), jnp.sum(guided * guided)), "seq")
    entries = own_vel.shape[0] * image_total
    rms_cond = jnp.sqrt(cond_sq / entries + EPS_NORM)
    rms_guided = jnp.sqrt(guided_sq / entries + EPS_NORM)
    result_vel = 0.7 * (guided * (rms_cond / rms_guided)) + 0.3 * guided
    channel_half = latents.shape[1]
    channel_start = lax.axis_index("cfg") * channel_half
    own_channels = lax.dynamic_slice_in_dim(result_vel, channel_start, channel_half, 0)
    next_index = jnp.minimum(step_index[0] + step_count[0], STEPS)
    step_size = sigma_of(next_index) - sigma_of(step_index[0])
    moved = latents[0] + step_size * own_channels
    return (own_channels[None], moved[None])


def solution(mesh):
    in_specs = (
        P("cfg", "req", "seq", None),
        P("cfg", "req", "seq", None),
        P("cfg", "req", None, None),
        P(None, "seq"),
        P(),
        P(None, "seq"),
        P("seq", None),
        P(),
        P("req", "cfg", "seq"),
        P("req"),
        P("cfg", "req"),
        P("req"),
        P("req"),
    )
    out_specs = (P("req", "cfg", "seq"), P("req", "cfg", "seq"))
    return jax.shard_map(local, mesh=mesh, in_specs=in_specs, out_specs=out_specs, check_vma=False)
```

profile of v0, /device:TPU:2, one launch (start us, length us, event | category | flops | bytes accessed | tf_op | source)
XLA Modules:
  0.0 735.5 jit_solution(12399066604961495987)
XLA Ops:
  10.6 1.6 slice_reduce_fusion.2
  16.3 210.6 %all-gather.3.cloned.1.call-done = bf16[1536,5120]{0,1:T(8,128)(2,1)} async-done(((bf16[1536,320]{0,1:T(8,128)(2,1)}), bf16[1536,5120]{0,1:T(8,128)(2,1)}) %all-gather.3.cloned.1.call-update) | async-done | bytes 15728656 | tf_op jit(solution)/shard_map/all_gather | solution.py:66
  226.9 8.3 %slice.78 = bf16[1536,16,3,64]{0,3,2,1:T(8,128)(2,1)} slice(bf16[1536,16,5,64]{0,3,2,1:T(8,128)(2,1)} %bitcast.100), slice={[0:1536], [0:16], [0:3], [0:64]} | slice | bytes 18874368 | tf_op jit(solution)/shard_map/slice | solution.py:36
  235.2 3.5 slice.81
  238.8 1.7 convolution_convert_fusion.2
  241.2 4.5 all-to-all-start.1
  245.8 7.8 %convolution_convert_fusion.1 = bf16[128,3072]{1,0:T(8,128)(2,1)} fusion(bf16[1536,3072]{0,1:T(8,128)(2,1)} %bitcast.98, bf16[1,1,128,1536]{3,2,1,0:T(8,128)(2,1)S(1)} %copy-done.3, f32[1536]{0:T(1024)} %get-tuple-element.58, f32[1536]{0:T(1024)} %get-tuple-element.59, f32[128]{0:T(128)} %add_rsqrt_fusion.3, f32[128]{0:T(128)} %copy-done.12), kind=kOutput, calls=%fused_computation.18 | convolution fusion | flops 1209532416 | bytes 10630144 | tf_op jit(solution)/shard_map/dot_general | solution.py:67
  253.6 2.3 copy.24
  256.4 9.1 %all-to-all-start = ((bf16[128,16,192]{0,2,1:T(8,128)(2,1)}), bf16[128,16,192]{0,2,1:T(8,128)(2,1)}, u32[]{:S(2)}, u32[]{:S(2)}) async-start(bf16[128,16,192]{0,2,1:T(8,128)(2,1)} %bitcast.102), calls=%async_computation | async-start | bytes 1572864 | tf_op jit(solution)/shard_map/all_to_all | solution.py:76
  267.5 21.1 %all-to-all-done = bf16[128,16,192]{0,2,1:T(8,128)(2,1)} async-done(((bf16[128,16,192]{0,2,1:T(8,128)(2,1)}), bf16[128,16,192]{0,2,1:T(8,128)(2,1)}, u32[]{:S(2)}, u32[]{:S(2)}) %all-to-all-start) | async-done | bytes 786464 | tf_op jit(solution)/shard_map/all_to_all | solution.py:76
  288.6 2.5 copy.25
  291.2 2.1 reshape.237
  293.3 2.0 slice_bitcast_fusion
  297.2 1.8 pad_maximum_fusion
  299.0 17.0 %while.10 = (s32[]{:T(128)}, bf16[4,512,1,64]{1,3,2,0:T(8,128)(2,1)}, pred[2208]{0:T(1024)(128)(4,1)S(1)}, bf16[4,512,1,64]{1,3,2,0:T(8,128)(2,1)}, bf16[2208,1,...) while((s32[]{:T(128)}, bf16[4,512,1,64]{1,3,2,0:T(8,128)(2,1)}, ...), condition=%wide.region_7.8_spmd, body=%wide.region_4.7_spmd.sunk | while | flops 297384960 | bytes 15406345 | solution.py:106
  299.0 1.9 fusion.95
  301.8 1.4 fusion.97
  303.3 1.8 fusion.95
  306.1 1.4 fusion.97
  307.5 1.8 fusion.95
  310.3 1.4 fusion.97
  311.8 1.8 fusion.95
  314.6 1.4 fusion.97
  319.0 16.4 %all_to_all.51 = bf16[16,128,64]{1,2,0:T(8,128)(2,1)S(1)} all-to-all(bf16[16,128,64]{1,2,0:T(8,128)(2,1)S(1)} %copy.31), channel_id=1, replica_groups=mesh['cfg'=2,'req'=8,'seq'=16] {'seq'}, dimensions={0} | all-to-all | bytes 524288 | tf_op jit(solution)/shard_map/all_to_all | solution.py:107
  335.4 1.7 fusion.76
  339.3 110.8 %all-gather.5.cloned.1.call-done = bf16[2048,1536]{1,0:T(8,128)(2,1)} async-done(((bf16[128,1536]{1,0:T(8,128)(2,1)}), bf16[2048,1536]{1,0:T(8,128)(2,1)}) %all-gather.5.cloned.1.call-update) | async-done | bytes 6291472 | tf_op jit(solution)/shard_map/all_gather | solution.py:112
  450.1 11.5 %convolution_convert_fusion = bf16[2048,1536]{1,0:T(8,128)(2,1)} fusion(bf16[384,1536]{1,0:T(8,128)(2,1)} %param.21, bf16[2048,1536]{1,0:T(8,128)(2,1)} %all-gather.5.cloned.1.call-done, bf16[1536,384]{1,0:T(8,128)(2,1)} %param.20), kind=kOutput, calls=%fused_computation.16 | convolution fusion | flops 4842061824 | bytes 14942208 | tf_op jit(solution)/shard_map/dot_general | solution.py:117
  461.6 216.7 %reduce-scatter.2.cloned.1.call-done = bf16[128,1536]{1,0:T(8,128)(2,1)} async-done(((bf16[2048,1536]{1,0:T(8,128)(2,1)}), bf16[128,1536]{1,0:T(8,128)(2,1)}) %reduce-scatter.2.cloned.1.call-update) | async-done | bytes 393232 | tf_op jit(solution)/shard_map/reduce_scatter | solution.py:116
  678.3 1.4 fusion.54
  679.8 1.5 multiply_reduce_fusion
  681.3 1.6 fusion.77
  687.3 39.7 %all-reduce.1 = (f32[]{:T(128)}, f32[]{:T(128)}) all-reduce(f32[]{:T(128)} %get-tuple-element.86, f32[]{:T(128)} %get-tuple-element.77), channel_id=1, replica_groups=mesh['cfg'=2,'req'=8,'seq'=16] {'seq'}, use_global_device_ids=true, to_apply=%region_14.15 | all-reduce | flops 2 | bytes 16 | tf_op jit(solution)/shard_map/psum | solution.py:132
  (84 shorter events, 23.8 us)
Async XLA Ops:
  7.2 328.3 %copy-start = (bf16[1024,1536]{1,0:T(8,128)(2,1)S(1)}, bf16[1024,1536]{1,0:T(8,128)(2,1)}, u32[]{:S(2)}) copy-start(bf16[1024,1536]{1,0:T(8,128)(2,1)} %param.19) | copy-start | bytes 9437188
  7.2 219.8 %all-gather.3.cloned.1.call-start = ((), (), s32[]{:S(2)}) async-start(), calls=%async_computation.4 | async-start | bytes 16711680 | tf_op jit(solution)/shard_map/all_gather | solution.py:66
  9.0 0.6 copy-start.13
  13.4 0.6 copy-start.12
  235.2 3.5 copy-start.4
  235.2 3.5 copy-start.7
  235.2 3.6 copy-start.8
  235.2 3.6 copy-start.14
  235.2 3.6 copy-start.15
  238.8 6.9 copy-start.3
  241.2 15.1 %all-to-all-start.1 = ((bf16[10,16,128]{2,0,1:T(8,128)(2,1)}), bf16[10,16,128]{2,0,1:T(8,128)(2,1)}, u32[]{:S(2)}, u32[]{:S(2)}) async-start(bf16[10,16,128]{2,0,1:T(8,128)(2,1)} %copy.26), calls=%async_computation.1 | async-start | bytes 131072 | tf_op jit(solution)/shard_map/all_to_all | solution.py:77
  256.4 32.3 %all-to-all-start = ((bf16[128,16,192]{0,2,1:T(8,128)(2,1)}), bf16[128,16,192]{0,2,1:T(8,128)(2,1)}, u32[]{:S(2)}, u32[]{:S(2)}) async-start(bf16[128,16,192]{0,2,1:T(8,128)(2,1)} %bitcast.102), calls=%async_computation | async-start | bytes 1572864 | tf_op jit(solution)/shard_map/all_to_all | solution.py:76
  265.5 184.6 %all-gather.5.cloned.1.call-start = ((), (), s32[]{:S(2)}) async-start(), calls=%async_computation.5 | async-start | bytes 6684672 | tf_op jit(solution)/shard_map/all_gather | solution.py:112
  299.0 36.4 %copy-start.6 = (f32[1536]{0:T(1024)S(1)}, f32[1536]{0:T(1024)}, u32[]{:S(2)}) copy-start(f32[1536]{0:T(1024)} %get-tuple-element.60) | copy-start | bytes 18436
  300.8 1.0 copy-start.2
  305.1 1.0 copy-start.2
  309.4 1.0 copy-start.2
  313.6 1.0 copy-start.2
  318.0 20.1 %copy-start.5 = (f32[1536]{0:T(1024)S(1)}, f32[1536]{0:T(1024)}, u32[]{:S(2)}) copy-start(f32[1536]{0:T(1024)} %get-tuple-element.55) | copy-start | bytes 18436
  337.1 0.9 copy-start.1
  339.1 339.3 %reduce-scatter.2.cloned.1.call-start = ((), (), s32[]{:S(2)}) async-start(), calls=%async_computation.6 | async-start | bytes 6684672 | tf_op jit(solution)/shard_map/reduce_scatter | solution.py:116
  461.6 219.7 %copy-start.10 = (f32[1536]{0:T(1024)S(1)}, f32[1536]{0:T(1024)}, u32[]{:S(2)}) copy-start(f32[1536]{0:T(1024)} %get-tuple-element.61) | copy-start | bytes 18436
  461.6 219.7 %copy-start.11 = (f32[1536]{0:T(1024)S(1)}, f32[1536]{0:T(1024)}, u32[]{:S(2)}) copy-start(f32[1536]{0:T(1024)} %get-tuple-element.62) | copy-start | bytes 18436
  461.6 219.7 %copy-start.16 = (bf16[64,1536]{1,0:T(8,128)(2,1)S(1)}, bf16[64,1536]{1,0:T(8,128)(2,1)}, u32[]{:S(2)}) copy-start(bf16[64,1536]{1,0:T(8,128)(2,1)} %param.22) | copy-start | bytes 589828
  461.6 266.8 %copy-start.9 = (f32[1,32,128]{2,1,0:T(8,128)S(1)}, f32[1,32,128]{2,1,0:T(8,128)}, u32[]{:S(2)}) copy-start(f32[1,32,128]{2,1,0:T(8,128)} %param.23) | copy-start | bytes 49156
  682.9 3.8 collective-permute-start
Sparse Core Ops, SparseCore 0:
  10.6 216.2 all-gather.2
  339.2 110.8 all-gather.4
  461.7 216.5 reduce-scatter.1
where the time goes:
time: 737 us; the launch traced here: 736 us
  waiting for transfers between devices  562 us (76%)
  blocking collectives  56.1 us (8%)
  matrix products  37.5 us (5%)
  local copies, waits for them, and re-layouts  30.5 us (4%)
  between operations  18.1 us (2%)
  other arithmetic  17.1 us (2%)
  starting transfers between devices  14.7 us (2%)
    reduce_scatter x1, waiting for transfers between devices, local(): lax.psum_scatter(jnp.dot(inner, mlp_out_weight, preferred_element_type=jn...  217 us
    all_gather x1, waiting for transfers between devices, local(): lax.all_gather(attn_weight, 'seq', axis=1, tiled=True)  211 us
    all_gather x1, waiting for transfers between devices, local(): mlp_all = lax.all_gather(mlp_norm, 'seq', axis=0, tiled=True)  111 us
    psum x1, blocking collectives, local(): lax.psum((jnp.sum(cond_vel * cond_vel), jnp.sum(guided * guided)), 'seq')  39.7 us
    all_to_all x1, waiting for transfers between devices, local(): lax.all_to_all(image_qkv, 'seq', split_axis=1, concat_axis=0, tiled=True)  21.1 us
    all_to_all x1, blocking collectives, local(): lax.all_to_all(attended, 'seq', split_axis=0, concat_axis=1, tiled=True)  16.4 us
  transfers between devices with their start and end apart: 6, of which 6 were waited for; matrix products, arithmetic and copies ran while one was open for 3% of the time, Pallas kernels for 0%

commit v1 on v0

--- a/solution.py
+++ b/solution.py
@@ -109,7 +109,9 @@
         attended, proj_weight, preferred_element_type=jnp.float32
     )
     mlp_norm = modulate(hidden, mod_rows[8], mod_rows[7])
-    mlp_all = lax.all_gather(mlp_norm, "seq", axis=0, tiled=True)
+    mlp_all = jnp.concatenate(
+        lax.all_to_all(jnp.stack([mlp_norm] * lax.axis_size("seq")), "seq", 0, 0), axis=0
+    )
     inner = jax.nn.gelu(
         jnp.dot(mlp_all, mlp_in_weight, preferred_element_type=jnp.float32), approximate=True
     ).astype(jnp.bfloat16)

time: 737 us -> 768 us (1.042)
  blocking collectives: 56.1 us -> 200 us
  waiting for transfers between devices: 562 us -> 450 us
    all_to_all x0 -> x1, blocking collectives: none -> 144 us  [local(): lax.all_to_all(jnp.stack([mlp_norm] * lax.axis_size('seq')), 'seq', 0, 0)]
    all_gather x1 -> x0, waiting for transfers between devices: 111 us -> none  [local(): mlp_all = lax.all_gather(mlp_norm, 'seq', axis=0, tiled=True)]
  transfers between devices with their start and end apart: 6 -> 5, of which waited for: 6 -> 5; matrix products, arithmetic and copies ran while one was open for 3% -> 2% of each run, Pallas kernels for 0% -> 0%
where the time goes in v1:
time: 768 us; the launch traced here: 767 us
  waiting for transfers between devices  450 us (59%)
  blocking collectives  200 us (26%)
  matrix products  37.8 us (5%)
  local copies, waits for them, and re-layouts  30 us (4%)
  between operations  18.4 us (2%)
  other arithmetic  16.3 us (2%)
  starting transfers between devices  14.4 us (2%)
    reduce_scatter x1, waiting for transfers between devices, local(): lax.psum_scatter(jnp.dot(inner, mlp_out_weight, preferred_element_type=jn...  216 us
    all_gather x1, waiting for transfers between devices, local(): lax.all_gather(attn_weight, 'seq', axis=1, tiled=True)  211 us
    all_to_all x1, blocking collectives, local(): lax.all_to_all(jnp.stack([mlp_norm] * lax.axis_size('seq')), 'seq', 0, 0)  144 us
    psum x1, blocking collectives, local(): lax.psum((jnp.sum(cond_vel * cond_vel), jnp.sum(guided * guided)), 'seq')  39.7 us
    all_to_all x1, waiting for transfers between devices, local(): lax.all_to_all(image_qkv, 'seq', split_axis=1, concat_axis=0, tiled=True)  21.1 us
    all_to_all x1, blocking collectives, local(): lax.all_to_all(attended, 'seq', split_axis=0, concat_axis=1, tiled=True)  16.4 us
  transfers between devices with their start and end apart: 5, of which 5 were waited for; matrix products, arithmetic and copies ran while one was open for 2% of the time, Pallas kernels for 0%

profile of v1, /device:TPU:2, one launch (start us, length us, event | category | flops | bytes accessed | tf_op | source)
XLA Modules:
  0.0 767.0 jit_solution(16850300318109841181)
XLA Ops:
  10.6 1.6 slice_reduce_fusion.2
  16.3 210.6 %all-gather.2.cloned.1.call-done = bf16[1536,5120]{0,1:T(8,128)(2,1)} async-done(((bf16[1536,320]{0,1:T(8,128)(2,1)}), bf16[1536,5120]{0,1:T(8,128)(2,1)}) %all-gather.2.cloned.1.call-update) | async-done | bytes 15728656 | tf_op jit(solution)/shard_map/all_gather | solution.py:66
  226.9 8.3 %slice.78 = bf16[1536,16,3,64]{0,3,2,1:T(8,128)(2,1)} slice(bf16[1536,16,5,64]{0,3,2,1:T(8,128)(2,1)} %bitcast.101), slice={[0:1536], [0:16], [0:3], [0:64]} | slice | bytes 18874368 | tf_op jit(solution)/shard_map/slice | solution.py:36
  235.2 3.5 slice.81
  238.8 1.7 convolution_convert_fusion.2
  241.2 4.5 all-to-all-start.1
  245.8 7.8 %convolution_convert_fusion.1 = bf16[128,3072]{1,0:T(8,128)(2,1)} fusion(bf16[1536,3072]{0,1:T(8,128)(2,1)} %bitcast.99, bf16[1,1,128,1536]{3,2,1,0:T(8,128)(2,1)S(1)} %copy-done.3, f32[1536]{0:T(1024)} %get-tuple-element.58, f32[1536]{0:T(1024)} %get-tuple-element.59, f32[128]{0:T(128)} %add_rsqrt_fusion.3, f32[128]{0:T(128)} %copy-done.12), kind=kOutput, calls=%fused_computation.18 | convolution fusion | flops 1209532416 | bytes 10630144 | tf_op jit(solution)/shard_map/dot_general | solution.py:67
  253.6 2.3 copy.24
  256.4 9.1 %all-to-all-start = ((bf16[128,16,192]{0,2,1:T(8,128)(2,1)}), bf16[128,16,192]{0,2,1:T(8,128)(2,1)}, u32[]{:S(2)}, u32[]{:S(2)}) async-start(bf16[128,16,192]{0,2,1:T(8,128)(2,1)} %bitcast.104), calls=%async_computation | async-start | bytes 1572864 | tf_op jit(solution)/shard_map/all_to_all | solution.py:76
  267.5 21.1 %all-to-all-done = bf16[128,16,192]{0,2,1:T(8,128)(2,1)} async-done(((bf16[128,16,192]{0,2,1:T(8,128)(2,1)}), bf16[128,16,192]{0,2,1:T(8,128)(2,1)}, u32[]{:S(2)}, u32[]{:S(2)}) %all-to-all-start) | async-done | bytes 786464 | tf_op jit(solution)/shard_map/all_to_all | solution.py:76
  288.6 2.5 copy.25
  291.2 2.1 reshape.242
  293.3 2.0 slice_bitcast_fusion
  297.2 1.8 pad_maximum_fusion
  299.0 16.1 %while.10 = (s32[]{:T(128)}, bf16[4,512,1,64]{1,3,2,0:T(8,128)(2,1)}, pred[2208]{0:T(1024)(128)(4,1)S(1)}, bf16[4,512,1,64]{1,3,2,0:T(8,128)(2,1)}, bf16[2208,1,...) while((s32[]{:T(128)}, bf16[4,512,1,64]{1,3,2,0:T(8,128)(2,1)}, ...), condition=%wide.region_7.8_spmd, body=%wide.region_4.7_spmd.sunk | while | flops 297384960 | bytes 15406345 | solution.py:106
  299.0 1.9 fusion.95
  301.6 1.5 fusion.97
  303.0 1.9 fusion.95
  305.6 1.5 fusion.97
  307.0 1.9 fusion.95
  309.6 1.4 fusion.97
  311.1 1.9 fusion.95
  313.6 1.4 fusion.97
  318.1 16.4 %all_to_all.56 = bf16[16,128,64]{1,2,0:T(8,128)(2,1)S(1)} all-to-all(bf16[16,128,64]{1,2,0:T(8,128)(2,1)S(1)} %copy.31), channel_id=1, replica_groups=mesh['cfg'=2,'req'=8,'seq'=16] {'seq'}, dimensions={0} | all-to-all | bytes 524288 | tf_op jit(solution)/shard_map/all_to_all | solution.py:107
  334.5 1.7 fusion.76
  337.9 144.4 %all_to_all.57 = bf16[16,128,1536]{2,1,0:T(8,128)(2,1)} all-to-all(bf16[16,128,1536]{2,1,0:T(8,128)(2,1)S(1)} %stack.2), channel_id=1, replica_groups=mesh['cfg'=2,'req'=8,'seq'=16] {'seq'}, dimensions={0} | all-to-all | bytes 12582912 | tf_op jit(solution)/shard_map/all_to_all | solution.py:113
  482.3 11.6 %convolution_convert_fusion = bf16[2048,1536]{1,0:T(8,128)(2,1)} fusion(bf16[384,1536]{1,0:T(8,128)(2,1)} %param.21, bf16[2048,1536]{1,0:T(8,128)(2,1)} %bitcast.103, bf16[1536,384]{1,0:T(8,128)(2,1)} %param.20), kind=kOutput, calls=%fused_computation.16 | convolution fusion | flops 4842061824 | bytes 14942208 | tf_op jit(solution)/shard_map/dot_general | solution.py:119
  493.9 215.5 %reduce-scatter.2.cloned.1.call-done = bf16[128,1536]{1,0:T(8,128)(2,1)} async-done(((bf16[2048,1536]{1,0:T(8,128)(2,1)}), bf16[128,1536]{1,0:T(8,128)(2,1)}) %reduce-scatter.2.cloned.1.call-update) | async-done | bytes 393232 | tf_op jit(solution)/shard_map/reduce_scatter | solution.py:118
  709.4 1.4 fusion.54
  710.9 1.5 multiply_reduce_fusion
  712.4 1.6 fusion.77
  718.4 39.7 %all-reduce.1 = (f32[]{:T(128)}, f32[]{:T(128)}) all-reduce(f32[]{:T(128)} %get-tuple-element.86, f32[]{:T(128)} %get-tuple-element.77), channel_id=1, replica_groups=mesh['cfg'=2,'req'=8,'seq'=16] {'seq'}, use_global_device_ids=true, to_apply=%region_14.15 | all-reduce | flops 2 | bytes 16 | tf_op jit(solution)/shard_map/psum | solution.py:134
  (83 shorter events, 22.3 us)
Async XLA Ops:
  7.2 327.3 %copy-start = (bf16[1024,1536]{1,0:T(8,128)(2,1)S(1)}, bf16[1024,1536]{1,0:T(8,128)(2,1)}, u32[]{:S(2)}) copy-start(bf16[1024,1536]{1,0:T(8,128)(2,1)} %param.19) | copy-start | bytes 9437188
  7.2 219.8 %all-gather.2.cloned.1.call-start = ((), (), s32[]{:S(2)}) async-start(), calls=%async_computation.5 | async-start | bytes 16711680 | tf_op jit(solution)/shard_map/all_gather | solution.py:66
  9.0 0.6 copy-start.13
  13.4 0.6 copy-start.12
  235.2 3.5 copy-start.4
  235.2 3.6 copy-start.7
  235.2 3.6 copy-start.8
  235.2 3.6 copy-start.14
  235.2 3.6 copy-start.15
  238.8 7.0 copy-start.3
  241.2 15.1 %all-to-all-start.1 = ((bf16[10,16,128]{2,0,1:T(8,128)(2,1)}), bf16[10,16,128]{2,0,1:T(8,128)(2,1)}, u32[]{:S(2)}, u32[]{:S(2)}) async-start(bf16[10,16,128]{2,0,1:T(8,128)(2,1)} %copy.26), calls=%async_computation.1 | async-start | bytes 131072 | tf_op jit(solution)/shard_map/all_to_all | solution.py:77
  256.4 32.3 %all-to-all-start = ((bf16[128,16,192]{0,2,1:T(8,128)(2,1)}), bf16[128,16,192]{0,2,1:T(8,128)(2,1)}, u32[]{:S(2)}, u32[]{:S(2)}) async-start(bf16[128,16,192]{0,2,1:T(8,128)(2,1)} %bitcast.104), calls=%async_computation | async-start | bytes 1572864 | tf_op jit(solution)/shard_map/all_to_all | solution.py:76
  265.5 443.9 %reduce-scatter.2.cloned.1.call-start = ((), (), s32[]{:S(2)}) async-start(), calls=%async_computation.6 | async-start | bytes 6684672 | tf_op jit(solution)/shard_map/reduce_scatter | solution.py:118
  299.0 35.5 %copy-start.6 = (f32[1536]{0:T(1024)S(1)}, f32[1536]{0:T(1024)}, u32[]{:S(2)}) copy-start(f32[1536]{0:T(1024)} %get-tuple-element.60) | copy-start | bytes 18436
  299.0 2.6 copy-start.2
  303.0 2.6 copy-start.2
  307.0 2.6 copy-start.2
  311.1 2.6 copy-start.2
  315.1 22.0 %copy-start.5 = (f32[1536]{0:T(1024)S(1)}, f32[1536]{0:T(1024)}, u32[]{:S(2)}) copy-start(f32[1536]{0:T(1024)} %get-tuple-element.55) | copy-start | bytes 18436
  336.2 0.9 copy-start.1
  493.9 218.5 %copy-start.10 = (f32[1536]{0:T(1024)S(1)}, f32[1536]{0:T(1024)}, u32[]{:S(2)}) copy-start(f32[1536]{0:T(1024)} %get-tuple-element.61) | copy-start | bytes 18436
  493.9 218.5 %copy-start.11 = (f32[1536]{0:T(1024)S(1)}, f32[1536]{0:T(1024)}, u32[]{:S(2)}) copy-start(f32[1536]{0:T(1024)} %get-tuple-element.62) | copy-start | bytes 18436
  493.9 218.5 %copy-start.16 = (bf16[64,1536]{1,0:T(8,128)(2,1)S(1)}, bf16[64,1536]{1,0:T(8,128)(2,1)}, u32[]{:S(2)}) copy-start(bf16[64,1536]{1,0:T(8,128)(2,1)} %param.22) | copy-start | bytes 589828
  493.9 265.6 %copy-start.9 = (f32[1,32,128]{2,1,0:T(8,128)S(1)}, f32[1,32,128]{2,1,0:T(8,128)}, u32[]{:S(2)}) copy-start(f32[1,32,128]{2,1,0:T(8,128)} %param.23) | copy-start | bytes 49156
  714.0 3.8 collective-permute-start
Sparse Core Ops, SparseCore 0:
  10.6 216.2 all-gather.1
  494.0 215.3 reduce-scatter.1
